TPU v7x, 32 devices: a whole 2x2x4 slice. The times are simulated.
32 devices in a mesh: ctx: 8 (over y, x, core), exp: 4 (over z).
Axes of the slice: x: 2, y: 2, z: 4, core: 2. Of those that a mesh axis runs over, the one named last changes fastest.
Arguments:
- inputs: bfloat16 [1024, 1024], P('exp', 'ctx'), may hold values from -6 to 6
- conv_taps: float32 [1024, 31], P('exp'), may hold values from -1 to 1
- norm_gain: bfloat16 [1024], P('exp'), may hold values from 0.099609375 to 1.8984375
- routes: int32 [1024, 2], P('ctx'), may hold values from 0 to 7, all different within a row; in each aligned block of 128 rows (0 to 127, 128 to 255, ...) at most 32 rows name the same one
- gate_probs: float32 [1024, 2], P('ctx'), may hold values from 0.1 to 0.9
- w_gate: bfloat16 [8, 1024, 4096], P('ctx', None, 'exp'), may hold values from -0.1875 to 0.1875
- w_up: bfloat16 [8, 1024, 4096], P('ctx', None, 'exp'), may hold values from -0.1875 to 0.1875
- w_down: bfloat16 [8, 4096, 1024], P('ctx', 'exp'), may hold values from -0.09375 to 0.09375
- grad_out: bfloat16 [1024, 1024], P('exp', 'ctx'), may hold values from -6 to 6
Outputs:
- layer_out: bfloat16 [1024, 1024], P('exp', 'ctx')
- grad_inputs: bfloat16 [1024, 1024], P('exp', 'ctx')
- grad_taps: float32 [1024, 31], P('exp')
- grad_gain: float32 [1024], P('exp')
- grad_gates: float32 [1024, 2], P('ctx')
- grad_w_gate: bfloat16 [8, 1024, 4096], P('ctx', None, 'exp')
- grad_w_up: bfloat16 [8, 1024, 4096], P('ctx', None, 'exp')
- grad_w_down: bfloat16 [8, 4096, 1024], P('ctx', 'exp')
Inputs may be any that keep to these rules, and one draw needn't show every extreme that they name: `routes`: in each aligned block of 128 rows (the rows of one index of ctx) no expert is named by more than 32 rows, a bound that some block reaches; the two experts of a row differ.
All inputs are finite; a program needn't handle non-finite values.
Results may differ from a plain program's by a relative error of at most 0.025.
Values may be sent and summed in bfloat16 or wider, within the bound.
A program may use at most 64 MiB of HBM per device.

v0:
```python
import jax
import jax.numpy as jnp
from jax import lax
from jax.sharding import PartitionSpec as P

EPS = 1e-05


def padded_2(cells, sides, width):
    for axis, dim in sides:
        count = lax.axis_size(axis)
        head = lax.slice_in_dim(cells, 0, width, axis=dim)
        tail = lax.slice_in_dim(cells, cells.shape[dim] - width, cells.shape[dim], axis=dim)
        cells = jnp.concatenate(
            [
                lax.ppermute(tail, axis, [(i, (i + 1) % count) for i in range(count)]),
                cells,
                lax.ppermute(head, axis, [((i + 1) % count, i) for i in range(count)]),
            ],
            axis=dim,
        )
    return cells


def shortened(x):

    def short(part):
        return part.astype(jnp.bfloat16) if part.dtype == jnp.float32 else part

    return jax.tree.map(short, x)


def slot_rows(routes, experts, capacity):
    flat = routes.reshape(-1)
    onehot = (flat[:, None] == jnp.arange(experts, dtype=jnp.int32)[None, :]).astype(jnp.int32)
    before = jnp.cumsum(onehot, axis=0, dtype=jnp.int32) - onehot
    place = jnp.sum(before * onehot, axis=1, dtype=jnp.int32)
    return flat * capacity + place


def bring_back(values, dest, weights, experts, capacity, whole_cot):
    width = values.shape[1]
    back = lax.all_to_all(
        values.reshape(experts, capacity, width).astype(jnp.bfloat16),
        "ctx",
        split_axis=0,
        concat_axis=0,
        tiled=True,
    ).astype(jnp.float32)
    picked = back.reshape(experts * capacity, width)[dest]
    term = jnp.sum((picked * weights[:, None]).reshape(-1, 2, width), axis=1)
    share = lax.psum_scatter(
        term.astype(jnp.bfloat16), "exp", scatter_dimension=1, tiled=True
    ).astype(jnp.float32)
    dots = None if whole_cot is None else jnp.sum(picked * whole_cot, axis=1)
    return (share, dots)


def local(inputs, conv_taps, norm_gain, routes, gate_probs, w_gate, w_up, w_down, grad_out):
    chans, tokens = inputs.shape
    taps = conv_taps.shape[1]
    half = taps // 2
    width = w_gate.shape[1]
    experts = lax.axis_size("ctx")
    capacity = max(tokens // 8, (2 * tokens + experts - 1) // experts)
    padded = padded_2(inputs, (("ctx", 1),), half)
    padded_f = padded.astype(jnp.float32)
    conv = jnp.zeros((chans, tokens), jnp.float32)
    for offset in range(taps):
        conv = conv + conv_taps[:, offset : offset + 1] * padded_f[:, offset : offset + tokens]
    mixed = (inputs.astype(jnp.float32) + conv).astype(jnp.bfloat16)
    mixed_f = mixed.astype(jnp.float32)
    gain_f = norm_gain.astype(jnp.float32)
    squares = lax.psum(jnp.sum(mixed_f * mixed_f, axis=0), "exp")
    scale = lax.rsqrt(squares / width + EPS)
    normed_part = (mixed_f * gain_f[:, None] * scale[None, :]).astype(jnp.bfloat16)
    normed, cotangent = (
        lax.all_gather(normed_part, "exp", axis=0, tiled=True),
        lax.all_gather(grad_out, "exp", axis=0, tiled=True),
    )
    dest = slot_rows(routes, experts, capacity)
    gates = gate_probs.reshape(-1)
    cot_rows = jnp.repeat(cotangent.T, 2, axis=0).astype(jnp.float32)
    token_rows = jnp.repeat(normed.T, 2, axis=0)
    scaled_rows = (cot_rows * gates[:, None]).astype(jnp.bfloat16)
    empty = jnp.zeros((experts * capacity, width), jnp.bfloat16)
    send_x = empty.at[dest].set(token_rows).reshape(experts, capacity, width)
    send_dy = empty.at[dest].set(scaled_rows).reshape(experts, capacity, width)
    recv_x, recv_dy = (
        lax.all_to_all(send_x, "ctx", split_axis=0, concat_axis=0, tiled=True),
        lax.all_to_all(send_dy, "ctx", split_axis=0, concat_axis=0, tiled=True),
    )
    rows_x = recv_x.reshape(-1, width)
    rows_dy = recv_dy.reshape(-1, width)
    weight_gate = w_gate[0]
    weight_up = w_up[0]
    weight_down = w_down[0]
    gate_act = jnp.dot(rows_x, weight_gate, preferred_element_type=jnp.float32)
    up_act = jnp.dot(rows_x, weight_up, preferred_element_type=jnp.float32)
    sigma = jax.nn.sigmoid(gate_act)
    hidden = (gate_act * sigma * up_act).astype(jnp.bfloat16)
    partial_out = jnp.dot(hidden, weight_down, preferred_element_type=jnp.float32)
    moe_share, gate_dots = bring_back(partial_out, dest, gates, experts, capacity, cot_rows)
    layer_out = (mixed_f + moe_share.T).astype(jnp.bfloat16)
    grad_gates = lax.psum(gate_dots, "exp").reshape(tokens, 2)
    contract_last = (((1,), (1,)), ((), ()))
    contract_first = (((0,), (0,)), ((), ()))
    d_hidden = lax.dot_general(
        rows_dy, weight_down, contract_last, preferred_element_type=jnp.float32
    )
    grad_down = lax.dot_general(
        hidden, rows_dy, contract_first, preferred_element_type=jnp.float32
    ).astype(jnp.bfloat16)
    d_gate = (d_hidden * up_act * sigma * (1.0 + gate_act * (1.0 - sigma))).astype(jnp.bfloat16)
    d_up = (d_hidden * gate_act * sigma).astype(jnp.bfloat16)
    grad_gate = lax.dot_general(
        rows_x, d_gate, contract_first, preferred_element_type=jnp.float32
    ).astype(jnp.bfloat16)
    grad_up = lax.dot_general(
        rows_x, d_up, contract_first, preferred_element_type=jnp.float32
    ).astype(jnp.bfloat16)
    d_rows = lax.dot_general(d_gate, weight_gate, contract_last, preferred_element_type=jnp.float32)
    d_rows = d_rows + lax.dot_general(
        d_up, weight_up, contract_last, preferred_element_type=jnp.float32
    )
    d_share, unused_dots = bring_back(d_rows, dest, jnp.ones_like(gates), experts, capacity, None)
    d_normed = d_share.T
    gain_local = jnp.sum(d_normed * mixed_f * scale[None, :], axis=1)
    norm_terms = lax.psum(jnp.sum(d_normed * gain_f[:, None] * mixed_f, axis=0), "exp")
    cot_own = grad_out.astype(jnp.float32)
    d_mixed = (
        cot_own
        + gain_f[:, None] * d_normed * scale[None, :]
        - mixed_f * (norm_terms * scale * scale * scale / width)[None, :]
    )
    grad_padded = padded_2(shortened(d_mixed), (("ctx", 1),), half).astype(d_mixed.dtype)
    grad_in = d_mixed
    tap_parts = []
    for offset in range(taps):
        grad_in = (
            grad_in
            + conv_taps[:, offset : offset + 1]
            * grad_padded[:, 2 * half - offset : 2 * half - offset + tokens]
        )
        tap_parts.append(jnp.sum(d_mixed * padded_f[:, offset : offset + tokens], axis=1))
    tap_local = jnp.stack(tap_parts, axis=1)
    grad_taps, grad_gain = lax.psum((tap_local, gain_local), "ctx")
    return (
        layer_out,
        grad_in.astype(jnp.bfloat16),
        grad_taps,
        grad_gain,
        grad_gates,
        grad_gate[None],
        grad_up[None],
        grad_down[None],
    )


def solution(mesh):
    return jax.shard_map(
        local,
        mesh=mesh,
        in_specs=(
            P("exp", "ctx"),
            P("exp", None),
            P("exp"),
            P("ctx", None),
            P("ctx", None),
            P("ctx", None, "exp"),
            P("ctx", None, "exp"),
            P("ctx", "exp", None),
            P("exp", "ctx"),
        ),
        out_specs=(
            P("exp", "ctx"),
            P("exp", "ctx"),
            P("exp", None),
            P("exp"),
            P("ctx", None),
            P("ctx", None, "exp"),
            P("ctx", None, "exp"),
            P("ctx", "exp", None),
        ),
        check_vma=False,
    )
```

profile of v0, /device:TPU:0, one launch (start us, length us, event | category | flops | bytes accessed | tf_op | source)
XLA Modules:
  0.0 213.7 jit_solution(18306011151170475799)
XLA Ops:
  8.8 2.9 %collective-permute-start.1 = (bf16[256,15]{0,1:T(8,128)(2,1)S(1)}, bf16[256,15]{0,1:T(8,128)(2,1)S(1)}, u32[]{:S(2)}, u32[]{:S(2)}) collective-permute-start(bf16[256,15]{0,1:T(8,128)(2,1)S(1)} %get-tuple-element.72), channel_id=1, source_target_pairs={{4,0},{8,4},{12,8},{16,12},{20,16},{24,20},{28,24},{0,28},{5,1},{9... | collective-permute-start | bytes 23048 | tf_op jit(solution)/shard_map/ppermute | solution.py:18
  15.5 15.0 %all_gather.7 = bf16[1024,128]{1,0:T(8,128)(2,1)S(1)} all-gather(bf16[256,128]{1,0:T(8,128)(2,1)} %param.17), channel_id=1, replica_groups=mesh['ctx'=8,'exp'=4] {'exp'}, dimensions={0}, use_global_device_ids=true | all-gather | bytes 327680 | tf_op jit(solution)/shard_map/all_gather | solution.py:79
  32.1 1.9 convert_element_type.108
  34.2 2.5 %scatter_custom_fusion.1 = bf16[256,1024]{1,0:T(8,128)(2,1)} fusion(s32[256]{0:T(256)S(1)} %bitcast.245, f32[256,1024]{1,0:T(8,128)S(1)} %convert_element_type.108, f32[256]{0:T(256)S(1)} %mul.828, bf16[]{:T(256)} %constant.8.clone.1), kind=kCustom, calls=%fused_computation.29 | custom fusion | flops 524288 | bytes 1573890 | tf_op jit(solution)/shard_map/scatter | solution.py:88
  36.7 4.1 %all-to-all-start.2 = ((bf16[8,32,1024]{2,1,0:T(8,128)(2,1)}), bf16[8,32,1024]{2,1,0:T(8,128)(2,1)}, u32[]{:S(2)}, u32[]{:S(2)}) async-start(bf16[8,32,1024]{2,1,0:T(8,128)(2,1)} %bitcast.149), calls=%async_computation.3 | async-start | bytes 1048576 | tf_op jit(solution)/shard_map/all_to_all | solution.py:91
  42.4 11.9 %psum.35 = f32[128]{0:T(128)S(1)} all-reduce(f32[128]{0:T(128)} %get-tuple-element.62), channel_id=1, replica_groups=mesh['ctx'=8,'exp'=4] {'exp'}, use_global_device_ids=true, to_apply=%region_4.5 | all-reduce | flops 128 | bytes 1024 | tf_op jit(solution)/shard_map/psum | solution.py:74
  54.9 13.8 %all_gather.6 = bf16[1024,128]{0,1:T(8,128)(2,1)S(1)} all-gather(bf16[256,128]{0,1:T(8,128)(2,1)S(1)} %fusion.27), channel_id=1, replica_groups=mesh['ctx'=8,'exp'=4] {'exp'}, dimensions={0}, use_global_device_ids=true | all-gather | bytes 327680 | tf_op jit(solution)/shard_map/all_gather | solution.py:78
  69.2 2.6 %scatter_custom_fusion = bf16[256,1024]{1,0:T(8,128)(2,1)} fusion(s32[256]{0:T(256)} %bitcast.246, bf16[256,1024]{1,0:T(8,128)(2,1)S(1)} %reshape.158, bf16[]{:T(256)} %constant.8.clone.1), kind=kCustom, calls=%fused_computation.41 | custom fusion | bytes 524800 | tf_op jit(solution)/shard_map/scatter | solution.py:87
  71.8 4.1 %all-to-all-start = ((bf16[8,32,1024]{2,1,0:T(8,128)(2,1)}), bf16[8,32,1024]{2,1,0:T(8,128)(2,1)S(1)}, u32[]{:S(2)}, u32[]{:S(2)}) async-start(bf16[8,32,1024]{2,1,0:T(8,128)(2,1)} %bitcast.36), calls=%async_computation | async-start | bytes 1048576 | tf_op jit(solution)/shard_map/all_to_all | solution.py:90
  76.5 3.5 %fusion.2 = f32[256,1024]{1,0:T(8,128)} fusion(bf16[256,1024]{1,0:T(8,128)(2,1)} %bitcast.47, bf16[1,1024,1024]{2,1,0:T(8,128)(2,1)} %param.16), kind=kOutput, calls=%fused_computation.6 | convolution fusion | flops 536870912 | bytes 3670016 | tf_op jit(solution)/shard_map/dot_general | solution.py:108
  80.0 5.6 %all-to-all-done = bf16[8,32,1024]{2,1,0:T(8,128)(2,1)S(1)} async-done(((bf16[8,32,1024]{2,1,0:T(8,128)(2,1)}), bf16[8,32,1024]{2,1,0:T(8,128)(2,1)S(1)}, u32[]{:S(2)}, u32[]{:S(2)}) %all-to-all-start) | async-done | bytes 524320 | tf_op jit(solution)/shard_map/all_to_all | solution.py:90
  85.6 2.5 %fusion.6 = f32[256,1024]{1,0:T(8,128)S(1)} fusion(bf16[256,1024]{1,0:T(8,128)(2,1)S(1)} %bitcast.145, bf16[1,1024,1024]{2,1,0:T(8,128)(2,1)} %param.15), kind=kOutput, calls=%fused_computation.10 | convolution fusion | flops 536870912 | bytes 3670016 | tf_op jit(solution)/shard_map/dot_general | solution.py:99
  88.1 2.0 multiply_convert_fusion.1
  90.9 1.5 fusion.15
  92.5 3.5 %all-to-all-start.1 = ((bf16[8,32,1024]{2,1,0:T(8,128)(2,1)}), bf16[8,32,1024]{2,1,0:T(8,128)(2,1)S(1)}, u32[]{:S(2)}, u32[]{:S(2)}) async-start(bf16[8,32,1024]{2,1,0:T(8,128)(2,1)} %fusion.15), calls=%async_computation.1 | async-start | bytes 1048576 | tf_op jit(solution)/shard_map/all_to_all | solution.py:43
  96.0 2.4 %fusion.4 = f32[256,1024]{1,0:T(8,128)S(1)} fusion(bf16[256,1024]{1,0:T(8,128)(2,1)S(1)} %get-tuple-element.66, bf16[1,1024,1024]{2,1,0:T(8,128)(2,1)} %param.15), kind=kOutput, calls=%fused_computation.8 | convolution fusion | flops 536870912 | bytes 3670016 | tf_op jit(solution)/shard_map/dot_general | solution.py:123
  98.4 1.6 fusion.18
  100.0 5.7 %all-to-all-done.1 = bf16[8,32,1024]{2,1,0:T(8,128)(2,1)S(1)} async-done(((bf16[8,32,1024]{2,1,0:T(8,128)(2,1)}), bf16[8,32,1024]{2,1,0:T(8,128)(2,1)S(1)}, u32[]{:S(2)}, u32[]{:S(2)}) %all-to-all-start.1) | async-done | bytes 524320 | tf_op jit(solution)/shard_map/all_to_all | solution.py:43
  105.6 4.2 %all-to-all-start.3 = ((bf16[8,32,1024]{2,1,0:T(8,128)(2,1)}), bf16[8,32,1024]{2,1,0:T(8,128)(2,1)}, u32[]{:S(2)}, u32[]{:S(2)}) async-start(bf16[8,32,1024]{2,1,0:T(8,128)(2,1)} %bitcast.48), calls=%async_computation.4 | async-start | bytes 1048576 | tf_op jit(solution)/shard_map/all_to_all | solution.py:43
  111.2 2.1 gather_fusion
  113.3 2.9 %gather.9 = f32[128,2,1024]{2,1,0:T(2,128)} reshape(f32[256,1024]{1,0:T(8,128)} %gather_fusion) | data formatting | bytes 2097152 | tf_op jit(solution)/shard_map/gather | solution.py:50
  116.2 3.3 %multiply_reduce_fusion.1 = bf16[128,1024]{1,0:T(8,128)(2,1)} fusion(f32[128,2,1024]{2,1,0:T(2,128)} %gather.9, f32[128,2]{1,0:T(8,128)S(1)} %copy.35), kind=kLoop, calls=%fused_computation.26 | loop fusion | flops 393216 | bytes 1311744 | tf_op jit(solution)/shard_map/reduce_sum | solution.py:51
  119.7 2.1 convert_bitcast_fusion.2
  123.0 2.0 gather_fusion.1
  125.0 2.9 %reshape.132 = f32[128,2,1024]{2,1,0:T(2,128)} reshape(f32[256,1024]{1,0:T(8,128)} %gather_fusion.1) | data formatting | bytes 2097152 | tf_op jit(solution)/shard_map/reshape | solution.py:51
  127.9 3.2 %reduce_sum.348 = bf16[128,1024]{1,0:T(8,128)(2,1)} reduce(f32[128,2,1024]{2,1,0:T(2,128)} %reshape.132, f32[]{:T(128)} %constant.7.clone.1), dimensions={1}, to_apply=%region_9.10 | reduce | flops 131072 | bytes 1310724 | tf_op jit(solution)/shard_map/reduce_sum | solution.py:51
  131.1 2.1 convert_bitcast_fusion.1
  133.2 3.3 %convert_bitcast_fusion = bf16[1,1024,1024]{2,1,0:T(8,128)(2,1)} fusion(bf16[256,1024]{1,0:T(8,128)(2,1)S(1)} %copy-done.15, bf16[256,1024]{1,0:T(8,128)(2,1)} %bitcast.47), kind=kOutput, calls=%fused_computation.16 | convolution fusion | flops 537919488 | bytes 3145728 | tf_op jit(solution)/shard_map/dot_general | solution.py:111
  137.8 20.4 %reduce-scatter.5.cloned.1.call-done = bf16[128,256]{1,0:T(8,128)(2,1)} async-done(((bf16[128,1024]{1,0:T(8,128)(2,1)}), bf16[128,256]{1,0:T(8,128)(2,1)}) %reduce-scatter.5.cloned.1.call-update) | async-done | bytes 65552 | tf_op jit(solution)/shard_map/reduce_scatter | solution.py:52
  159.1 17.2 %all-reduce.1 = (f32[128]{0:T(128)S(1)}, f32[128,2]{1,0:T(8,128)S(1)}) all-reduce(f32[128]{0:T(128)S(1)} %get-tuple-element.56, f32[128,2]{1,0:T(8,128)S(1)} %reshape.133), channel_id=1, replica_groups=mesh['ctx'=8,'exp'=4] {'exp'}, use_global_device_ids=true, to_apply=%region_12.13 | all-reduce | flops 384 | bytes 3072 | tf_op jit(solution)/shard_map/psum | solution.py:129
  178.1 2.6 %collective-permute-start.3 = (bf16[256,15]{0,1:T(8,128)(2,1)S(1)}, bf16[256,15]{0,1:T(8,128)(2,1)S(1)}, u32[]{:S(2)}, u32[]{:S(2)}) collective-permute-start(bf16[256,15]{0,1:T(8,128)(2,1)S(1)} %get-tuple-element.69), channel_id=1, source_target_pairs={{4,0},{8,4},{12,8},{16,12},{20,16},{24,20},{28,24},{0,28},{5,1},{9... | collective-permute-start | bytes 23048 | tf_op jit(solution)/shard_map/ppermute | solution.py:18
  180.8 23.3 %all-reduce = (f32[256,31]{0,1:T(8,128)}, f32[256]{0:T(256)}) all-reduce(f32[256,31]{0,1:T(8,128)S(1)} %stack.127, f32[256]{0:T(256)S(1)} %get-tuple-element.55), channel_id=1, replica_groups=mesh['ctx'=8,'exp'=4] {'ctx'}, use_global_device_ids=true, to_apply=%region_44.45 | all-reduce | flops 8192 | bytes 65536 | tf_op jit(solution)/shard_map/psum | solution.py:147
  (191 shorter events, 20.0 us)
Async XLA Ops:
  7.2 81.0 %copy-start = (bf16[1,1024,1024]{2,1,0:T(8,128)(2,1)S(1)}, bf16[1,1024,1024]{2,1,0:T(8,128)(2,1)}, u32[]{:S(2)}) copy-start(bf16[1,1024,1024]{2,1,0:T(8,128)(2,1)} %param.14) | copy-start | bytes 6291460
  8.3 32.8 %collective-permute-start = (bf16[256,15]{0,1:T(8,128)(2,1)S(1)}, bf16[256,15]{0,1:T(8,128)(2,1)S(1)}, u32[]{:S(2)}, u32[]{:S(2)}) collective-permute-start(bf16[256,15]{0,1:T(8,128)(2,1)S(1)} %get-tuple-element.71), channel_id=1, source_target_pairs={{0,4},{4,8},{8,12},{12,16},{16,20},{20,24},{24,28},{28,0},{1,5},{5... | collective-permute-start | bytes 23048 | tf_op jit(solution)/shard_map/ppermute | solution.py:16
  8.8 32.4 %collective-permute-start.1 = (bf16[256,15]{0,1:T(8,128)(2,1)S(1)}, bf16[256,15]{0,1:T(8,128)(2,1)S(1)}, u32[]{:S(2)}, u32[]{:S(2)}) collective-permute-start(bf16[256,15]{0,1:T(8,128)(2,1)S(1)} %get-tuple-element.72), channel_id=1, source_target_pairs={{4,0},{8,4},{12,8},{16,12},{20,16},{24,20},{28,24},{0,28},{5,1},{9... | collective-permute-start | bytes 23048 | tf_op jit(solution)/shard_map/ppermute | solution.py:18
  36.7 35.1 %all-to-all-start.2 = ((bf16[8,32,1024]{2,1,0:T(8,128)(2,1)}), bf16[8,32,1024]{2,1,0:T(8,128)(2,1)}, u32[]{:S(2)}, u32[]{:S(2)}) async-start(bf16[8,32,1024]{2,1,0:T(8,128)(2,1)} %bitcast.149), calls=%async_computation.3 | async-start | bytes 1048576 | tf_op jit(solution)/shard_map/all_to_all | solution.py:91
  71.8 13.8 %all-to-all-start = ((bf16[8,32,1024]{2,1,0:T(8,128)(2,1)}), bf16[8,32,1024]{2,1,0:T(8,128)(2,1)S(1)}, u32[]{:S(2)}, u32[]{:S(2)}) async-start(bf16[8,32,1024]{2,1,0:T(8,128)(2,1)} %bitcast.36), calls=%async_computation | async-start | bytes 1048576 | tf_op jit(solution)/shard_map/all_to_all | solution.py:90
  92.5 13.2 %all-to-all-start.1 = ((bf16[8,32,1024]{2,1,0:T(8,128)(2,1)}), bf16[8,32,1024]{2,1,0:T(8,128)(2,1)S(1)}, u32[]{:S(2)}, u32[]{:S(2)}) async-start(bf16[8,32,1024]{2,1,0:T(8,128)(2,1)} %fusion.15), calls=%async_computation.1 | async-start | bytes 1048576 | tf_op jit(solution)/shard_map/all_to_all | solution.py:43
  105.6 16.2 %all-to-all-start.3 = ((bf16[8,32,1024]{2,1,0:T(8,128)(2,1)}), bf16[8,32,1024]{2,1,0:T(8,128)(2,1)}, u32[]{:S(2)}, u32[]{:S(2)}) async-start(bf16[8,32,1024]{2,1,0:T(8,128)(2,1)} %bitcast.48), calls=%async_computation.4 | async-start | bytes 1048576 | tf_op jit(solution)/shard_map/all_to_all | solution.py:43
  109.8 27.9 %reduce-scatter.3.cloned.1.call-start = ((), (), s32[]{:S(2)}) async-start(), calls=%async_computation.6 | async-start | bytes 327680 | tf_op jit(solution)/shard_map/reduce_scatter | solution.py:52
  119.6 38.6 %reduce-scatter.5.cloned.1.call-start = ((), (), s32[]{:S(2)}) async-start(), calls=%async_computation.7 | async-start | bytes 327680 | tf_op jit(solution)/shard_map/reduce_scatter | solution.py:52
  133.2 43.1 %copy-start.65 = (f32[128]{0:T(128)S(1)}, f32[128]{0:T(128)}, u32[]{:S(2)}) copy-start(f32[128]{0:T(128)} %copy-done.64) | copy-start | bytes 1540
  176.4 29.1 %copy-start.19 = (f32[256,1]{0,1:T(1,128)S(1)}, f32[256,1]{0,1:T(1,128)}, u32[]{:S(2)}) copy-start(f32[256,1]{0,1:T(1,128)} %copy-done.18) | copy-start | bytes 3076
  176.4 29.1 %copy-start.21 = (f32[256,1]{0,1:T(1,128)S(1)}, f32[256,1]{0,1:T(1,128)}, u32[]{:S(2)}) copy-start(f32[256,1]{0,1:T(1,128)} %copy-done.20) | copy-start | bytes 3076
  176.4 29.1 %copy-start.23 = (f32[256,1]{0,1:T(1,128)S(1)}, f32[256,1]{0,1:T(1,128)}, u32[]{:S(2)}) copy-start(f32[256,1]{0,1:T(1,128)} %copy-done.22) | copy-start | bytes 3076
  176.4 29.1 %copy-start.25 = (f32[256,1]{0,1:T(1,128)S(1)}, f32[256,1]{0,1:T(1,128)}, u32[]{:S(2)}) copy-start(f32[256,1]{0,1:T(1,128)} %copy-done.24) | copy-start | bytes 3076
  176.4 29.1 %copy-start.27 = (f32[256,1]{0,1:T(1,128)S(1)}, f32[256,1]{0,1:T(1,128)}, u32[]{:S(2)}) copy-start(f32[256,1]{0,1:T(1,128)} %copy-done.26) | copy-start | bytes 3076
  176.4 29.1 %copy-start.29 = (f32[256,1]{0,1:T(1,128)S(1)}, f32[256,1]{0,1:T(1,128)}, u32[]{:S(2)}) copy-start(f32[256,1]{0,1:T(1,128)} %copy-done.28) | copy-start | bytes 3076
  176.4 29.1 %copy-start.31 = (f32[256,1]{0,1:T(1,128)S(1)}, f32[256,1]{0,1:T(1,128)}, u32[]{:S(2)}) copy-start(f32[256,1]{0,1:T(1,128)} %copy-done.30) | copy-start | bytes 3076
  176.4 29.1 %copy-start.33 = (f32[256,1]{0,1:T(1,128)S(1)}, f32[256,1]{0,1:T(1,128)}, u32[]{:S(2)}) copy-start(f32[256,1]{0,1:T(1,128)} %copy-done.32) | copy-start | bytes 3076
  176.4 29.1 %copy-start.35 = (f32[256,1]{0,1:T(1,128)S(1)}, f32[256,1]{0,1:T(1,128)}, u32[]{:S(2)}) copy-start(f32[256,1]{0,1:T(1,128)} %copy-done.34) | copy-start | bytes 3076
  176.5 29.1 %copy-start.37 = (f32[256,1]{0,1:T(1,128)S(1)}, f32[256,1]{0,1:T(1,128)}, u32[]{:S(2)}) copy-start(f32[256,1]{0,1:T(1,128)} %copy-done.36) | copy-start | bytes 3076
  176.5 29.1 %copy-start.39 = (f32[256,1]{0,1:T(1,128)S(1)}, f32[256,1]{0,1:T(1,128)}, u32[]{:S(2)}) copy-start(f32[256,1]{0,1:T(1,128)} %copy-done.38) | copy-start | bytes 3076
  176.5 29.1 %copy-start.41 = (f32[256,1]{0,1:T(1,128)S(1)}, f32[256,1]{0,1:T(1,128)}, u32[]{:S(2)}) copy-start(f32[256,1]{0,1:T(1,128)} %copy-done.40) | copy-start | bytes 3076
  176.5 29.1 %copy-start.43 = (f32[256,1]{0,1:T(1,128)S(1)}, f32[256,1]{0,1:T(1,128)}, u32[]{:S(2)}) copy-start(f32[256,1]{0,1:T(1,128)} %copy-done.42) | copy-start | bytes 3076
  176.5 29.1 %copy-start.45 = (f32[256,1]{0,1:T(1,128)S(1)}, f32[256,1]{0,1:T(1,128)}, u32[]{:S(2)}) copy-start(f32[256,1]{0,1:T(1,128)} %copy-done.44) | copy-start | bytes 3076
  176.5 29.1 %copy-start.47 = (f32[256,1]{0,1:T(1,128)S(1)}, f32[256,1]{0,1:T(1,128)}, u32[]{:S(2)}) copy-start(f32[256,1]{0,1:T(1,128)} %copy-done.46) | copy-start | bytes 3076
  176.5 29.1 %copy-start.49 = (f32[256,1]{0,1:T(1,128)S(1)}, f32[256,1]{0,1:T(1,128)}, u32[]{:S(2)}) copy-start(f32[256,1]{0,1:T(1,128)} %copy-done.48) | copy-start | bytes 3076
  176.5 29.1 %copy-start.51 = (f32[256,1]{0,1:T(1,128)S(1)}, f32[256,1]{0,1:T(1,128)}, u32[]{:S(2)}) copy-start(f32[256,1]{0,1:T(1,128)} %copy-done.50) | copy-start | bytes 3076
  176.5 29.1 %copy-start.53 = (f32[256,1]{0,1:T(1,128)S(1)}, f32[256,1]{0,1:T(1,128)}, u32[]{:S(2)}) copy-start(f32[256,1]{0,1:T(1,128)} %copy-done.52) | copy-start | bytes 3076
  176.5 29.1 %copy-start.55 = (f32[256,1]{0,1:T(1,128)S(1)}, f32[256,1]{0,1:T(1,128)}, u32[]{:S(2)}) copy-start(f32[256,1]{0,1:T(1,128)} %copy-done.54) | copy-start | bytes 3076
  176.6 29.1 %copy-start.57 = (f32[256,1]{0,1:T(1,128)S(1)}, f32[256,1]{0,1:T(1,128)}, u32[]{:S(2)}) copy-start(f32[256,1]{0,1:T(1,128)} %copy-done.56) | copy-start | bytes 3076
  178.0 27.5 %collective-permute-start.2 = (bf16[256,15]{0,1:T(8,128)(2,1)S(1)}, bf16[256,15]{0,1:T(8,128)(2,1)S(1)}, u32[]{:S(2)}, u32[]{:S(2)}) collective-permute-start(bf16[256,15]{0,1:T(8,128)(2,1)S(1)} %get-tuple-element.68), channel_id=1, source_target_pairs={{0,4},{4,8},{8,12},{12,16},{16,20},{20,24},{24,28},{28,0},{1,5},{5... | collective-permute-start | bytes 23048 | tf_op jit(solution)/shard_map/ppermute | solution.py:16
  178.1 27.4 %collective-permute-start.3 = (bf16[256,15]{0,1:T(8,128)(2,1)S(1)}, bf16[256,15]{0,1:T(8,128)(2,1)S(1)}, u32[]{:S(2)}, u32[]{:S(2)}) collective-permute-start(bf16[256,15]{0,1:T(8,128)(2,1)S(1)} %get-tuple-element.69), channel_id=1, source_target_pairs={{4,0},{8,4},{12,8},{16,12},{20,16},{24,20},{28,24},{0,28},{5,1},{9... | collective-permute-start | bytes 23048 | tf_op jit(solution)/shard_map/ppermute | solution.py:18
  (44 other events, 194.0 us)
Sparse Core Ops, SparseCore 0:
  119.7 18.0 reduce-scatter.2
  140.1 17.9 reduce-scatter.4
where the time goes:
time: 215 us; the launch traced here: 214 us
  blocking collectives  81.2 us (38%)
  waiting for transfers between devices  32.6 us (15%)
  local copies, waits for them, and re-layouts  24.1 us (11%)
  starting transfers between devices  22.3 us (10%)
  matrix products  20.8 us (10%)
  other arithmetic  17.6 us (8%)
  between operations  15.1 us (7%)
    psum x1, blocking collectives, local(): grad_taps, grad_gain = lax.psum((tap_local, gain_local), 'ctx')  23.3 us
    reduce_scatter x2, waiting for transfers between devices, bring_back(): lax.psum_scatter(term.astype(jnp.bfloat16), 'exp', scatter_dimension=1, t...  21.3 us
    psum x1, blocking collectives, local(): lax.psum(jnp.sum(d_normed * gain_f[:, None] * mixed_f, axis=0), 'exp')  17.2 us
    all_gather x1, blocking collectives, local(): lax.all_gather(grad_out, 'exp', axis=0, tiled=True)  15 us
    all_gather x1, blocking collectives, local(): lax.all_gather(normed_part, 'exp', axis=0, tiled=True)  13.8 us
    psum x1, blocking collectives, local(): squares = lax.psum(jnp.sum(mixed_f * mixed_f, axis=0), 'exp')  11.9 us
    all_to_all x2, starting transfers between devices, bring_back(): lax.all_to_all(values.reshape(experts, capacity, width).astype(jnp.bfloat...  7.65 us
    gather x3, local copies, waits for them, and re-layouts, bring_back(): picked = back.reshape(experts * capacity, width)[dest]  7 us
  transfers between devices with their start and end apart: 10, of which 4 were waited for; matrix products, arithmetic and copies ran while one was open for 23% of the time, Pallas kernels for 0%

commit v1 on v0

--- a/solution.py
+++ b/solution.py
@@ -86,8 +86,26 @@
     empty = jnp.zeros((experts * capacity, width), jnp.bfloat16)
     send_x = empty.at[dest].set(token_rows).reshape(experts, capacity, width)
     send_dy = empty.at[dest].set(scaled_rows).reshape(experts, capacity, width)
+
+    def fill_yards(z_in):
+        upper, frame_out = (jax.lax.psum(1, "ctx"), jax.lax.axis_index("ctx"))
+        local_next = z_in.shape[0] // upper
+        outer = list(z_in.shape)
+        outer[0] = local_next
+        t_next = outer[0]
+        outer[0] = t_next * upper
+        parts_out = jnp.zeros(outer, z_in.dtype)
+        for s in range(upper):
+            lower = lax.dynamic_slice_in_dim(z_in, (frame_out ^ s) * local_next, local_next, axis=0)
+            if s:
+                lower = jax.lax.ppermute(lower, "ctx", perm=[(i0, i0 ^ s) for i0 in range(upper)])
+            parts_out = lax.dynamic_update_slice_in_dim(
+                parts_out, lower, (frame_out ^ s) * t_next, axis=0
+            )
+        return parts_out
+
     recv_x, recv_dy = (
-        lax.all_to_all(send_x, "ctx", split_axis=0, concat_axis=0, tiled=True),
+        fill_yards(send_x),
         lax.all_to_all(send_dy, "ctx", split_axis=0, concat_axis=0, tiled=True),
     )
     rows_x = recv_x.reshape(-1, width)

time: 215 us -> 216 us (level)
  starting transfers between devices: 22.3 us -> 25.4 us
    ppermute x0 -> x7, starting transfers between devices: none -> 7.2 us  [fill_yards(): jax.lax.ppermute(lower, 'ctx', perm=[(i0, i0 ^ s) for i0 in range(upper)])]
    ppermute x0 -> x7, waiting for transfers between devices: none -> 6.39 us  [fill_yards(): jax.lax.ppermute(lower, 'ctx', perm=[(i0, i0 ^ s) for i0 in range(upper)])]
    all_to_all x1 -> x0, waiting for transfers between devices: 5.58 us -> none  [local(): lax.all_to_all(send_x, 'ctx', split_axis=0, concat_axis=0, tiled=True)]
    all_to_all x1 -> x0, starting transfers between devices: 4.09 us -> none  [local(): lax.all_to_all(send_x, 'ctx', split_axis=0, concat_axis=0, tiled=True)]
  transfers between devices with their start and end apart: 10 -> 16, of which waited for: 4 -> 5; matrix products, arithmetic and copies ran while one was open for 23% -> 22% of each run, Pallas kernels for 0% -> 0%
where the time goes in v1:
time: 216 us; the launch traced here: 215 us
  blocking collectives  81.1 us (38%)
  waiting for transfers between devices  33.6 us (16%)
  starting transfers between devices  25.4 us (12%)
  local copies, waits for them, and re-layouts  24.3 us (11%)
  matrix products  19.1 us (9%)
  other arithmetic  16.4 us (8%)
  between operations  15.3 us (7%)
    psum x1, blocking collectives, local(): grad_taps, grad_gain = lax.psum((tap_local, gain_local), 'ctx')  23.3 us
    reduce_scatter x2, waiting for transfers between devices, bring_back(): lax.psum_scatter(term.astype(jnp.bfloat16), 'exp', scatter_dimension=1, t...  21.4 us
    psum x1, blocking collectives, local(): lax.psum(jnp.sum(d_normed * gain_f[:, None] * mixed_f, axis=0), 'exp')  17.2 us
    all_gather x1, blocking collectives, local(): lax.all_gather(grad_out, 'exp', axis=0, tiled=True)  15 us
    all_gather x1, blocking collectives, local(): lax.all_gather(normed_part, 'exp', axis=0, tiled=True)  13.8 us
    psum x1, blocking collectives, local(): squares = lax.psum(jnp.sum(mixed_f * mixed_f, axis=0), 'exp')  11.8 us
    all_to_all x2, starting transfers between devices, bring_back(): lax.all_to_all(values.reshape(experts, capacity, width).astype(jnp.bfloat...  7.83 us
    ppermute x7, starting transfers between devices, fill_yards(): jax.lax.ppermute(lower, 'ctx', perm=[(i0, i0 ^ s) for i0 in range(upper)])  7.2 us
  transfers between devices with their start and end apart: 16, of which 5 were waited for; matrix products, arithmetic and copies ran while one was open for 22% of the time, Pallas kernels for 0%

profile of v1, /device:TPU:0, one launch (start us, length us, event | category | flops | bytes accessed | tf_op | source)
XLA Modules:
  0.0 215.2 jit_solution(8067262728108988700)
XLA Ops:
  8.8 2.9 %collective-permute-start.1 = (bf16[256,15]{0,1:T(8,128)(2,1)S(1)}, bf16[256,15]{0,1:T(8,128)(2,1)S(1)}, u32[]{:S(2)}, u32[]{:S(2)}) collective-permute-start(bf16[256,15]{0,1:T(8,128)(2,1)S(1)} %get-tuple-element.80), channel_id=1, source_target_pairs={{4,0},{8,4},{12,8},{16,12},{20,16},{24,20},{28,24},{0,28},{5,1},{9... | collective-permute-start | bytes 23048 | tf_op jit(solution)/shard_map/ppermute | solution.py:18
  15.5 15.0 %all_gather.7 = bf16[1024,128]{1,0:T(8,128)(2,1)S(1)} all-gather(bf16[256,128]{1,0:T(8,128)(2,1)} %param.17), channel_id=1, replica_groups=mesh['ctx'=8,'exp'=4] {'exp'}, dimensions={0}, use_global_device_ids=true | all-gather | bytes 327680 | tf_op jit(solution)/shard_map/all_gather | solution.py:79
  32.1 1.9 convert_element_type.108
  34.2 2.5 %scatter_custom_fusion.1 = bf16[256,1024]{1,0:T(8,128)(2,1)} fusion(s32[256]{0:T(256)S(1)} %bitcast.246, f32[256,1024]{1,0:T(8,128)S(1)} %convert_element_type.108, f32[256]{0:T(256)S(1)} %mul.828, bf16[]{:T(256)} %constant.18.clone.1), kind=kCustom, calls=%fused_computation.29 | custom fusion | flops 524288 | bytes 1573890 | tf_op jit(solution)/shard_map/scatter | solution.py:88
  36.7 4.1 %all-to-all-start.1 = ((bf16[8,32,1024]{2,1,0:T(8,128)(2,1)}), bf16[8,32,1024]{2,1,0:T(8,128)(2,1)}, u32[]{:S(2)}, u32[]{:S(2)}) async-start(bf16[8,32,1024]{2,1,0:T(8,128)(2,1)} %bitcast.149), calls=%async_computation.2 | async-start | bytes 1048576 | tf_op jit(solution)/shard_map/all_to_all | solution.py:109
  41.9 11.8 %psum.35 = f32[128]{0:T(128)S(1)} all-reduce(f32[128]{0:T(128)S(1)} %get-tuple-element.62), channel_id=1, replica_groups=mesh['ctx'=8,'exp'=4] {'exp'}, use_global_device_ids=true, to_apply=%region_4.5 | all-reduce | flops 128 | bytes 1024 | tf_op jit(solution)/shard_map/psum | solution.py:74
  53.8 13.8 %all_gather.6 = bf16[1024,128]{0,1:T(8,128)(2,1)S(1)} all-gather(bf16[256,128]{0,1:T(8,128)(2,1)S(1)} %fusion.27), channel_id=1, replica_groups=mesh['ctx'=8,'exp'=4] {'exp'}, dimensions={0}, use_global_device_ids=true | all-gather | bytes 327680 | tf_op jit(solution)/shard_map/all_gather | solution.py:78
  68.9 2.3 %scatter_custom_fusion = bf16[256,1024]{1,0:T(8,128)(2,1)S(1)} fusion(s32[256]{0:T(256)S(1)} %bitcast.247, bf16[256,1024]{1,0:T(8,128)(2,1)} %reshape.158, bf16[]{:T(256)} %constant.18.clone.1), kind=kCustom, calls=%fused_computation.41 | custom fusion | bytes 524800 | tf_op jit(solution)/shard_map/scatter | solution.py:87
  71.4 2.9 %collective-permute-start.8 = (bf16[1,32,1024]{2,1,0:T(8,128)(2,1)S(1)}, bf16[1,32,1024]{2,1,0:T(8,128)(2,1)S(1)}, u32[]{:S(2)}, u32[]{:S(2)}) collective-permute-start(bf16[1,32,1024]{2,1,0:T(8,128)(2,1)S(1)} %get-tuple-element.67), channel_id=1, source_target_pairs={{0,28},{4,24},{8,20},{12,16},{16,12},{20,8},{24,4},{28,0},{1,29},{... | collective-permute-start | bytes 196616 | tf_op jit(solution)/shard_map/ppermute | solution.py:101
  77.9 2.8 %collective-permute-done.3 = bf16[1,32,1024]{2,1,0:T(8,128)(2,1)S(1)} collective-permute-done((bf16[1,32,1024]{2,1,0:T(8,128)(2,1)S(1)}, bf16[1,32,1024]{2,1,0:T(8,128)(2,1)S(1)}, u32[]{:S(2)}, u32[]{:S(2)}) %collective-permute-start.3) | collective-permute-done | bytes 65568 | tf_op jit(solution)/shard_map/ppermute | solution.py:101
  81.4 3.6 %collective-permute-done.4 = bf16[1,32,1024]{2,1,0:T(8,128)(2,1)S(1)} collective-permute-done((bf16[1,32,1024]{2,1,0:T(8,128)(2,1)S(1)}, bf16[1,32,1024]{2,1,0:T(8,128)(2,1)S(1)}, u32[]{:S(2)}, u32[]{:S(2)}) %collective-permute-start.4) | collective-permute-done | bytes 65568 | tf_op jit(solution)/shard_map/ppermute | solution.py:101
  85.1 1.7 fusion.6
  86.8 2.6 %fusion.2 = f32[256,1024]{1,0:T(8,128)S(1)} fusion(bf16[256,1024]{1,0:T(8,128)(2,1)} %bitcast.47, bf16[1,1024,1024]{2,1,0:T(8,128)(2,1)} %param.16), kind=kOutput, calls=%fused_computation.6 | convolution fusion | flops 536870912 | bytes 3670016 | tf_op jit(solution)/shard_map/dot_general | solution.py:126
  89.4 2.0 multiply_convert_fusion.1
  93.7 3.7 %all-to-all-start = ((bf16[8,32,1024]{2,1,0:T(8,128)(2,1)}), bf16[8,32,1024]{2,1,0:T(8,128)(2,1)S(1)}, u32[]{:S(2)}, u32[]{:S(2)}) async-start(bf16[8,32,1024]{2,1,0:T(8,128)(2,1)} %fusion.15), calls=%async_computation | async-start | bytes 1048576 | tf_op jit(solution)/shard_map/all_to_all | solution.py:43
  97.4 2.4 %fusion.4 = f32[256,1024]{1,0:T(8,128)S(1)} fusion(bf16[256,1024]{1,0:T(8,128)(2,1)S(1)} %get-tuple-element.66, bf16[1,1024,1024]{2,1,0:T(8,128)(2,1)} %param.15), kind=kOutput, calls=%fused_computation.8 | convolution fusion | flops 536870912 | bytes 3670016 | tf_op jit(solution)/shard_map/dot_general | solution.py:141
  99.8 1.6 fusion.18
  101.4 5.7 %all-to-all-done = bf16[8,32,1024]{2,1,0:T(8,128)(2,1)S(1)} async-done(((bf16[8,32,1024]{2,1,0:T(8,128)(2,1)}), bf16[8,32,1024]{2,1,0:T(8,128)(2,1)S(1)}, u32[]{:S(2)}, u32[]{:S(2)}) %all-to-all-start) | async-done | bytes 524320 | tf_op jit(solution)/shard_map/all_to_all | solution.py:43
  107.2 4.2 %all-to-all-start.2 = ((bf16[8,32,1024]{2,1,0:T(8,128)(2,1)}), bf16[8,32,1024]{2,1,0:T(8,128)(2,1)}, u32[]{:S(2)}, u32[]{:S(2)}) async-start(bf16[8,32,1024]{2,1,0:T(8,128)(2,1)} %bitcast.48), calls=%async_computation.3 | async-start | bytes 1048576 | tf_op jit(solution)/shard_map/all_to_all | solution.py:43
  112.5 2.1 gather_fusion
  114.6 2.9 %gather.9 = f32[128,2,1024]{2,1,0:T(2,128)} reshape(f32[256,1024]{1,0:T(8,128)} %gather_fusion) | data formatting | bytes 2097152 | tf_op jit(solution)/shard_map/gather | solution.py:50
  117.5 3.3 %multiply_reduce_fusion.1 = bf16[128,1024]{1,0:T(8,128)(2,1)} fusion(f32[128,2,1024]{2,1,0:T(2,128)} %gather.9, f32[128,2]{1,0:T(8,128)S(1)} %copy.35), kind=kLoop, calls=%fused_computation.26 | loop fusion | flops 393216 | bytes 1311744 | tf_op jit(solution)/shard_map/reduce_sum | solution.py:51
  121.1 2.1 convert_bitcast_fusion.2
  124.3 2.0 gather_fusion.1
  126.3 2.9 %reshape.132 = f32[128,2,1024]{2,1,0:T(2,128)} reshape(f32[256,1024]{1,0:T(8,128)} %gather_fusion.1) | data formatting | bytes 2097152 | tf_op jit(solution)/shard_map/reshape | solution.py:51
  129.2 3.2 %reduce_sum.348 = bf16[128,1024]{1,0:T(8,128)(2,1)} reduce(f32[128,2,1024]{2,1,0:T(2,128)} %reshape.132, f32[]{:T(128)} %constant.8.clone.1), dimensions={1}, to_apply=%region_9.10 | reduce | flops 131072 | bytes 1310724 | tf_op jit(solution)/shard_map/reduce_sum | solution.py:51
  132.5 2.1 convert_bitcast_fusion.1
  134.6 3.3 %convert_bitcast_fusion = bf16[1,1024,1024]{2,1,0:T(8,128)(2,1)} fusion(bf16[256,1024]{1,0:T(8,128)(2,1)S(1)} %copy-done.16, bf16[256,1024]{1,0:T(8,128)(2,1)} %bitcast.47), kind=kOutput, calls=%fused_computation.16 | convolution fusion | flops 537919488 | bytes 3145728 | tf_op jit(solution)/shard_map/dot_general | solution.py:129
  139.3 20.2 %reduce-scatter.5.cloned.1.call-done = bf16[128,256]{1,0:T(8,128)(2,1)} async-done(((bf16[128,1024]{1,0:T(8,128)(2,1)}), bf16[128,256]{1,0:T(8,128)(2,1)}) %reduce-scatter.5.cloned.1.call-update) | async-done | bytes 65552 | tf_op jit(solution)/shard_map/reduce_scatter | solution.py:52
  160.6 17.2 %all-reduce.1 = (f32[128]{0:T(128)S(1)}, f32[128,2]{1,0:T(8,128)S(1)}) all-reduce(f32[128]{0:T(128)S(1)} %get-tuple-element.56, f32[128,2]{1,0:T(8,128)S(1)} %reshape.133), channel_id=1, replica_groups=mesh['ctx'=8,'exp'=4] {'exp'}, use_global_device_ids=true, to_apply=%region_12.13 | all-reduce | flops 384 | bytes 3072 | tf_op jit(solution)/shard_map/psum | solution.py:147
  179.5 2.6 %collective-permute-start.10 = (bf16[256,15]{0,1:T(8,128)(2,1)S(1)}, bf16[256,15]{0,1:T(8,128)(2,1)S(1)}, u32[]{:S(2)}, u32[]{:S(2)}) collective-permute-start(bf16[256,15]{0,1:T(8,128)(2,1)S(1)} %get-tuple-element.77), channel_id=1, source_target_pairs={{4,0},{8,4},{12,8},{16,12},{20,16},{24,20},{28,24},{0,28},{5,1},{9... | collective-permute-start | bytes 23048 | tf_op jit(solution)/shard_map/ppermute | solution.py:18
  182.3 23.3 %all-reduce = (f32[256,31]{0,1:T(8,128)}, f32[256]{0:T(256)}) all-reduce(f32[256,31]{0,1:T(8,128)S(1)} %stack.127, f32[256]{0:T(256)S(1)} %get-tuple-element.55), channel_id=1, replica_groups=mesh['ctx'=8,'exp'=4] {'ctx'}, use_global_device_ids=true, to_apply=%region_44.45 | all-reduce | flops 8192 | bytes 65536 | tf_op jit(solution)/shard_map/psum | solution.py:165
  (212 shorter events, 25.1 us)
Async XLA Ops:
  7.2 82.2 %copy-start = (bf16[1,1024,1024]{2,1,0:T(8,128)(2,1)S(1)}, bf16[1,1024,1024]{2,1,0:T(8,128)(2,1)}, u32[]{:S(2)}) copy-start(bf16[1,1024,1024]{2,1,0:T(8,128)(2,1)} %param.14) | copy-start | bytes 6291460
  8.3 32.9 %collective-permute-start = (bf16[256,15]{0,1:T(8,128)(2,1)S(1)}, bf16[256,15]{0,1:T(8,128)(2,1)S(1)}, u32[]{:S(2)}, u32[]{:S(2)}) collective-permute-start(bf16[256,15]{0,1:T(8,128)(2,1)S(1)} %get-tuple-element.79), channel_id=1, source_target_pairs={{0,4},{4,8},{8,12},{12,16},{16,20},{20,24},{24,28},{28,0},{1,5},{5... | collective-permute-start | bytes 23048 | tf_op jit(solution)/shard_map/ppermute | solution.py:16
  8.8 32.4 %collective-permute-start.1 = (bf16[256,15]{0,1:T(8,128)(2,1)S(1)}, bf16[256,15]{0,1:T(8,128)(2,1)S(1)}, u32[]{:S(2)}, u32[]{:S(2)}) collective-permute-start(bf16[256,15]{0,1:T(8,128)(2,1)S(1)} %get-tuple-element.80), channel_id=1, source_target_pairs={{4,0},{8,4},{12,8},{16,12},{20,16},{24,20},{28,24},{0,28},{5,1},{9... | collective-permute-start | bytes 23048 | tf_op jit(solution)/shard_map/ppermute | solution.py:18
  36.7 50.1 %all-to-all-start.1 = ((bf16[8,32,1024]{2,1,0:T(8,128)(2,1)}), bf16[8,32,1024]{2,1,0:T(8,128)(2,1)}, u32[]{:S(2)}, u32[]{:S(2)}) async-start(bf16[8,32,1024]{2,1,0:T(8,128)(2,1)} %bitcast.149), calls=%async_computation.2 | async-start | bytes 1048576 | tf_op jit(solution)/shard_map/all_to_all | solution.py:109
  71.3 5.1 %collective-permute-start.2 = (bf16[1,32,1024]{2,1,0:T(8,128)(2,1)S(1)}, bf16[1,32,1024]{2,1,0:T(8,128)(2,1)S(1)}, u32[]{:S(2)}, u32[]{:S(2)}) collective-permute-start(bf16[1,32,1024]{2,1,0:T(8,128)(2,1)S(1)} %get-tuple-element.73), channel_id=1, source_target_pairs={{0,4},{4,0},{8,12},{12,8},{16,20},{20,16},{24,28},{28,24},{1,5},{5... | collective-permute-start | bytes 196616 | tf_op jit(solution)/shard_map/ppermute | solution.py:101
  71.4 13.6 %collective-permute-start.8 = (bf16[1,32,1024]{2,1,0:T(8,128)(2,1)S(1)}, bf16[1,32,1024]{2,1,0:T(8,128)(2,1)S(1)}, u32[]{:S(2)}, u32[]{:S(2)}) collective-permute-start(bf16[1,32,1024]{2,1,0:T(8,128)(2,1)S(1)} %get-tuple-element.67), channel_id=1, source_target_pairs={{0,28},{4,24},{8,20},{12,16},{16,12},{20,8},{24,4},{28,0},{1,29},{... | collective-permute-start | bytes 196616 | tf_op jit(solution)/shard_map/ppermute | solution.py:101
  74.4 10.7 %collective-permute-start.7 = (bf16[1,32,1024]{2,1,0:T(8,128)(2,1)S(1)}, bf16[1,32,1024]{2,1,0:T(8,128)(2,1)S(1)}, u32[]{:S(2)}, u32[]{:S(2)}) collective-permute-start(bf16[1,32,1024]{2,1,0:T(8,128)(2,1)S(1)} %get-tuple-element.68), channel_id=1, source_target_pairs={{0,24},{4,28},{8,16},{12,20},{16,8},{20,12},{24,0},{28,4},{1,25},{... | collective-permute-start | bytes 196616 | tf_op jit(solution)/shard_map/ppermute | solution.py:101
  74.5 10.5 %collective-permute-start.6 = (bf16[1,32,1024]{2,1,0:T(8,128)(2,1)S(1)}, bf16[1,32,1024]{2,1,0:T(8,128)(2,1)S(1)}, u32[]{:S(2)}, u32[]{:S(2)}) collective-permute-start(bf16[1,32,1024]{2,1,0:T(8,128)(2,1)S(1)} %get-tuple-element.69), channel_id=1, source_target_pairs={{0,20},{4,16},{8,28},{12,24},{16,4},{20,0},{24,12},{28,8},{1,21},{... | collective-permute-start | bytes 196616 | tf_op jit(solution)/shard_map/ppermute | solution.py:101
  75.8 9.2 %collective-permute-start.5 = (bf16[1,32,1024]{2,1,0:T(8,128)(2,1)S(1)}, bf16[1,32,1024]{2,1,0:T(8,128)(2,1)S(1)}, u32[]{:S(2)}, u32[]{:S(2)}) collective-permute-start(bf16[1,32,1024]{2,1,0:T(8,128)(2,1)S(1)} %get-tuple-element.70), channel_id=1, source_target_pairs={{0,16},{4,20},{8,24},{12,28},{16,0},{20,4},{24,8},{28,12},{1,17},{... | collective-permute-start | bytes 196616 | tf_op jit(solution)/shard_map/ppermute | solution.py:101
  76.4 4.3 %collective-permute-start.3 = (bf16[1,32,1024]{2,1,0:T(8,128)(2,1)S(1)}, bf16[1,32,1024]{2,1,0:T(8,128)(2,1)S(1)}, u32[]{:S(2)}, u32[]{:S(2)}) collective-permute-start(bf16[1,32,1024]{2,1,0:T(8,128)(2,1)S(1)} %get-tuple-element.72), channel_id=1, source_target_pairs={{0,8},{4,12},{8,0},{12,4},{16,24},{20,28},{24,16},{28,20},{1,9},{5... | collective-permute-start | bytes 196616 | tf_op jit(solution)/shard_map/ppermute | solution.py:101
  80.7 4.3 %collective-permute-start.4 = (bf16[1,32,1024]{2,1,0:T(8,128)(2,1)S(1)}, bf16[1,32,1024]{2,1,0:T(8,128)(2,1)S(1)}, u32[]{:S(2)}, u32[]{:S(2)}) collective-permute-start(bf16[1,32,1024]{2,1,0:T(8,128)(2,1)S(1)} %get-tuple-element.71), channel_id=1, source_target_pairs={{0,12},{4,8},{8,4},{12,0},{16,28},{20,24},{24,20},{28,16},{1,13},{... | collective-permute-start | bytes 196616 | tf_op jit(solution)/shard_map/ppermute | solution.py:101
  93.7 13.4 %all-to-all-start = ((bf16[8,32,1024]{2,1,0:T(8,128)(2,1)}), bf16[8,32,1024]{2,1,0:T(8,128)(2,1)S(1)}, u32[]{:S(2)}, u32[]{:S(2)}) async-start(bf16[8,32,1024]{2,1,0:T(8,128)(2,1)} %fusion.15), calls=%async_computation | async-start | bytes 1048576 | tf_op jit(solution)/shard_map/all_to_all | solution.py:43
  107.2 16.0 %all-to-all-start.2 = ((bf16[8,32,1024]{2,1,0:T(8,128)(2,1)}), bf16[8,32,1024]{2,1,0:T(8,128)(2,1)}, u32[]{:S(2)}, u32[]{:S(2)}) async-start(bf16[8,32,1024]{2,1,0:T(8,128)(2,1)} %bitcast.48), calls=%async_computation.3 | async-start | bytes 1048576 | tf_op jit(solution)/shard_map/all_to_all | solution.py:43
  111.3 28.0 %reduce-scatter.3.cloned.1.call-start = ((), (), s32[]{:S(2)}) async-start(), calls=%async_computation.5 | async-start | bytes 327680 | tf_op jit(solution)/shard_map/reduce_scatter | solution.py:52
  120.9 38.7 %reduce-scatter.5.cloned.1.call-start = ((), (), s32[]{:S(2)}) async-start(), calls=%async_computation.6 | async-start | bytes 327680 | tf_op jit(solution)/shard_map/reduce_scatter | solution.py:52
  134.6 43.2 %copy-start.65 = (f32[128]{0:T(128)S(1)}, f32[128]{0:T(128)}, u32[]{:S(2)}) copy-start(f32[128]{0:T(128)} %copy-done.64) | copy-start | bytes 1540
  177.8 29.1 %copy-start.20 = (f32[256,1]{0,1:T(1,128)S(1)}, f32[256,1]{0,1:T(1,128)}, u32[]{:S(2)}) copy-start(f32[256,1]{0,1:T(1,128)} %copy-done.19) | copy-start | bytes 3076
  177.8 29.1 %copy-start.22 = (f32[256,1]{0,1:T(1,128)S(1)}, f32[256,1]{0,1:T(1,128)}, u32[]{:S(2)}) copy-start(f32[256,1]{0,1:T(1,128)} %copy-done.21) | copy-start | bytes 3076
  177.8 29.1 %copy-start.24 = (f32[256,1]{0,1:T(1,128)S(1)}, f32[256,1]{0,1:T(1,128)}, u32[]{:S(2)}) copy-start(f32[256,1]{0,1:T(1,128)} %copy-done.23) | copy-start | bytes 3076
  177.8 29.1 %copy-start.26 = (f32[256,1]{0,1:T(1,128)S(1)}, f32[256,1]{0,1:T(1,128)}, u32[]{:S(2)}) copy-start(f32[256,1]{0,1:T(1,128)} %copy-done.25) | copy-start | bytes 3076
  177.9 29.1 %copy-start.28 = (f32[256,1]{0,1:T(1,128)S(1)}, f32[256,1]{0,1:T(1,128)}, u32[]{:S(2)}) copy-start(f32[256,1]{0,1:T(1,128)} %copy-done.27) | copy-start | bytes 3076
  177.9 29.1 %copy-start.30 = (f32[256,1]{0,1:T(1,128)S(1)}, f32[256,1]{0,1:T(1,128)}, u32[]{:S(2)}) copy-start(f32[256,1]{0,1:T(1,128)} %copy-done.29) | copy-start | bytes 3076
  177.9 29.1 %copy-start.32 = (f32[256,1]{0,1:T(1,128)S(1)}, f32[256,1]{0,1:T(1,128)}, u32[]{:S(2)}) copy-start(f32[256,1]{0,1:T(1,128)} %copy-done.31) | copy-start | bytes 3076
  177.9 29.1 %copy-start.34 = (f32[256,1]{0,1:T(1,128)S(1)}, f32[256,1]{0,1:T(1,128)}, u32[]{:S(2)}) copy-start(f32[256,1]{0,1:T(1,128)} %copy-done.33) | copy-start | bytes 3076
  177.9 29.1 %copy-start.36 = (f32[256,1]{0,1:T(1,128)S(1)}, f32[256,1]{0,1:T(1,128)}, u32[]{:S(2)}) copy-start(f32[256,1]{0,1:T(1,128)} %copy-done.35) | copy-start | bytes 3076
  177.9 29.1 %copy-start.38 = (f32[256,1]{0,1:T(1,128)S(1)}, f32[256,1]{0,1:T(1,128)}, u32[]{:S(2)}) copy-start(f32[256,1]{0,1:T(1,128)} %copy-done.37) | copy-start | bytes 3076
  177.9 29.1 %copy-start.40 = (f32[256,1]{0,1:T(1,128)S(1)}, f32[256,1]{0,1:T(1,128)}, u32[]{:S(2)}) copy-start(f32[256,1]{0,1:T(1,128)} %copy-done.39) | copy-start | bytes 3076
  177.9 29.1 %copy-start.42 = (f32[256,1]{0,1:T(1,128)S(1)}, f32[256,1]{0,1:T(1,128)}, u32[]{:S(2)}) copy-start(f32[256,1]{0,1:T(1,128)} %copy-done.41) | copy-start | bytes 3076
  177.9 29.1 %copy-start.44 = (f32[256,1]{0,1:T(1,128)S(1)}, f32[256,1]{0,1:T(1,128)}, u32[]{:S(2)}) copy-start(f32[256,1]{0,1:T(1,128)} %copy-done.43) | copy-start | bytes 3076
  177.9 29.1 %copy-start.46 = (f32[256,1]{0,1:T(1,128)S(1)}, f32[256,1]{0,1:T(1,128)}, u32[]{:S(2)}) copy-start(f32[256,1]{0,1:T(1,128)} %copy-done.45) | copy-start | bytes 3076
  179.5 27.5 %collective-permute-start.9 = (bf16[256,15]{0,1:T(8,128)(2,1)S(1)}, bf16[256,15]{0,1:T(8,128)(2,1)S(1)}, u32[]{:S(2)}, u32[]{:S(2)}) collective-permute-start(bf16[256,15]{0,1:T(8,128)(2,1)S(1)} %get-tuple-element.76), channel_id=1, source_target_pairs={{0,4},{4,8},{8,12},{12,16},{16,20},{20,24},{24,28},{28,0},{1,5},{5... | collective-permute-start | bytes 23048 | tf_op jit(solution)/shard_map/ppermute | solution.py:16
  179.5 27.4 %collective-permute-start.10 = (bf16[256,15]{0,1:T(8,128)(2,1)S(1)}, bf16[256,15]{0,1:T(8,128)(2,1)S(1)}, u32[]{:S(2)}, u32[]{:S(2)}) collective-permute-start(bf16[256,15]{0,1:T(8,128)(2,1)S(1)} %get-tuple-element.77), channel_id=1, source_target_pairs={{4,0},{8,4},{12,8},{16,12},{20,16},{24,20},{28,24},{0,28},{5,1},{9... | collective-permute-start | bytes 23048 | tf_op jit(solution)/shard_map/ppermute | solution.py:18
  (50 other events, 383.8 us)
Sparse Core Ops, SparseCore 0:
  121.0 18.2 reduce-scatter.2
  141.7 17.8 reduce-scatter.4
